TPU v7x, 32 devices: a whole 2x2x4 slice. The times are simulated.
32 devices in a mesh: dp: 8 (over y, x, core), tensor: 4 (over z).
Axes of the slice: x: 2, y: 2, z: 4, core: 2. Of those that a mesh axis runs over, the one named last changes fastest.
Arguments:
- tokens: bfloat16 [4096, 768], P(('dp', 'tensor')), may hold values from -6 to 6
- gain_attn: float32 [768], replicated, may hold values from 0.5 to 1.5
- gain_ffn: float32 [768], replicated, may hold values from 0.5 to 1.5
- w_query: bfloat16 [768, 768], P('dp', 'tensor'), may hold values from -0.078125 to 0.078125
- w_key: bfloat16 [768, 768], P('dp', 'tensor'), may hold values from -0.21875 to 0.21875
- w_value: bfloat16 [768, 768], P('dp', 'tensor'), may hold values from -0.21875 to 0.21875
- w_output: bfloat16 [768, 768], P('dp', 'tensor'), may hold values from -0.875 to 0.875
- bias_table: float32 [32, 12], replicated, may hold values from -4 to 4
- router: float32 [768, 2], replicated, may hold values from -0.15625 to 0.15625
- w_in: bfloat16 [768, 2, 3072], P('dp', None, 'tensor'), may hold values from -0.21875 to 0.21875
- w_out: bfloat16 [768, 2, 3072], P('dp', None, 'tensor'), may hold values from -0.3125 to 0.3125
- routes: int32 [4096, 1], P('dp'), may hold values from 0 to 1; in each aligned block of 512 rows (0 to 511, 512 to 1023, ...) at most 384 rows name the same one
- lengths: int32 [8, 4], P('dp'), may hold values from 1 to 448, 512 in all within a row
- cotangent: bfloat16 [4096, 768], P(('dp', 'tensor')), may hold values from -6 to 6
Outputs:
- mixed_out: bfloat16 [4096, 768], P(('dp', 'tensor'))
- grad_tokens: float32 [4096, 768], P(('dp', 'tensor'))
- grad_gain_attn: float32 [768], replicated
- grad_gain_ffn: float32 [768], replicated
- grad_query: float32 [768, 768], P('dp', 'tensor')
- grad_key: float32 [768, 768], P('dp', 'tensor')
- grad_value: float32 [768, 768], P('dp', 'tensor')
- grad_output: float32 [768, 768], P('dp', 'tensor')
- grad_bias: float32 [32, 12], replicated
- grad_router: float32 [768, 2], replicated
- grad_in: float32 [768, 2, 3072], P('dp', None, 'tensor')
- grad_out: float32 [768, 2, 3072], P('dp', None, 'tensor')
Inputs may be any that keep to these rules, and one draw needn't show every extreme that they name: `routes`: in each group (aligned block of 512 tokens) no expert has more than 384 tokens. Each group's lengths sum to 512, and its longest is exactly 448.
All inputs are finite; a program needn't handle non-finite values.
Results may differ from a plain program's by a relative error of at most 0.017.
Values may be sent and summed in bfloat16 or wider, within the bound.
A program may use at most 128 MiB of HBM per device.

v0:
```python
import jax
import jax.numpy as jnp
from jax import lax
from jax.sharding import PartitionSpec as P

HEAD_DIM = 64
EXPERTS = 2
BUCKETS = 32


highest = lax.Precision.HIGHEST
bucket_edges = (12, 16, 23, 32, 46, 64, 91)


def rms_scale(values, gain):
    return values * lax.rsqrt(jnp.mean(values * values, axis=-1, keepdims=True) + 1e-06) * gain


def bucket_of(relative):
    distance = jnp.abs(relative)
    far_part = jnp.full(distance.shape, 8, jnp.int32)
    for edge in bucket_edges:
        far_part = far_part + (distance >= edge).astype(jnp.int32)
    return jnp.where(distance < 8, distance, far_part) + 16 * (relative > 0).astype(jnp.int32)


def position_buckets(length):
    position = jnp.arange(length, dtype=jnp.int32)
    return bucket_of(position[None, :] - position[:, None])


def diagonal_sums(values):
    rows = values.shape[0]
    padded = jnp.concatenate([jnp.zeros((rows, rows), jnp.float32), values], axis=1)
    flat = jnp.concatenate([padded.reshape(-1), jnp.zeros((rows,), jnp.float32)])
    skewed = flat.reshape(rows, 2 * rows + 1)
    return jnp.sum(skewed, axis=0)


def same_sequence(seq_lengths, length):
    position = jnp.arange(length, dtype=jnp.int32)
    ends = jnp.cumsum(seq_lengths)
    segment = jnp.sum((position[:, None] >= ends[None, :]).astype(jnp.int32), axis=1)
    return segment[:, None] == segment[None, :]


def expert_slots(route_ids, capacity):
    onehot = (route_ids[:, None] == jnp.arange(EXPERTS, dtype=jnp.int32)[None, :]).astype(jnp.int32)
    before = jnp.cumsum(onehot, axis=0) - onehot
    slot_of = jnp.sum(before * onehot, axis=1)
    counts = jnp.sum(onehot, axis=0)
    token_of = (
        jnp.zeros((EXPERTS, capacity), jnp.int32)
        .at[route_ids, slot_of]
        .set(jnp.arange(route_ids.shape[0], dtype=jnp.int32))
    )
    filled = jnp.arange(capacity, dtype=jnp.int32)[None, :] < counts[:, None]
    return (slot_of, token_of, filled)


def dot_nt(left, right):
    return lax.dot_general(
        left, right, (((1,), (1,)), ((), ())), preferred_element_type=jnp.float32
    )


def dot_tn(left, right):
    return lax.dot_general(
        left, right, (((0,), (0,)), ((), ())), preferred_element_type=jnp.float32
    )


def gelu_tanh(values):
    return jax.nn.gelu(values, approximate=True)


def on_device(
    tokens,
    gain_attn,
    gain_ffn,
    w_query,
    w_key,
    w_value,
    w_output,
    bias_table,
    router,
    w_in,
    w_out,
    routes,
    lengths,
    cotangent,
):
    tok_count = tokens.shape[0]
    tensor_at = lax.axis_index("tensor")
    group_rows = tok_count * lax.axis_size("tensor")
    capacity = 3 * group_rows // (2 * EXPERTS)
    head_count = w_query.shape[1] // HEAD_DIM
    head_width = w_query.shape[1]
    unit_width = w_in.shape[2]
    full_query, full_key, full_value, full_output = (
        lax.all_gather(w_query, "dp", axis=0, tiled=True),
        lax.all_gather(w_key, "dp", axis=0, tiled=True),
        lax.all_gather(w_value, "dp", axis=0, tiled=True),
        lax.all_gather(w_output, "dp", axis=0, tiled=True),
    )
    tok_f32 = tokens.astype(jnp.float32)
    normed = rms_scale(tok_f32, gain_attn).astype(jnp.bfloat16)
    gathered = lax.all_gather(normed, "tensor", axis=0, tiled=True)
    query = jnp.dot(gathered, full_query, preferred_element_type=jnp.float32).astype(jnp.bfloat16)
    key_proj = jnp.dot(gathered, full_key, preferred_element_type=jnp.float32).astype(jnp.bfloat16)
    value_proj = jnp.dot(gathered, full_value, preferred_element_type=jnp.float32).astype(
        jnp.bfloat16
    )
    same_seq = same_sequence(lengths[0], group_rows)
    bucket = position_buckets(group_rows)
    table_here = lax.dynamic_slice_in_dim(bias_table, tensor_at * head_count, head_count, 1)

    def head_scores(head_at):
        start_col = head_at * HEAD_DIM
        q_part = query[:, start_col : start_col + HEAD_DIM]
        k_part = key_proj[:, start_col : start_col + HEAD_DIM]
        scores = dot_nt(q_part, k_part) + jnp.take(table_here[:, head_at], bucket)
        return jnp.where(same_seq, scores, -1e30)

    head_outputs = []
    log_totals = []
    for head_at in range(head_count):
        scores = head_scores(head_at)
        top = jnp.max(scores, axis=-1, keepdims=True)
        weights = jnp.exp(scores - top)
        total = jnp.sum(weights, axis=-1, keepdims=True)
        log_totals.append(top[:, 0] + jnp.log(total[:, 0]))
        probs = (weights / total).astype(jnp.bfloat16)
        start_col = head_at * HEAD_DIM
        head_outputs.append(
            jnp.dot(
                probs,
                value_proj[:, start_col : start_col + HEAD_DIM],
                preferred_element_type=jnp.float32,
            )
        )
    attended = jnp.concatenate(head_outputs, axis=1).astype(jnp.bfloat16)
    branch = lax.psum_scatter(
        dot_nt(attended, full_output), "tensor", scatter_dimension=0, tiled=True
    )
    middle = tok_f32 + branch
    normed_ffn = rms_scale(middle, gain_ffn).astype(jnp.bfloat16)
    route_ids = routes[:, 0]
    own_routes = lax.dynamic_slice_in_dim(route_ids, tensor_at * tok_count, tok_count)
    own_onehot = (own_routes[:, None] == jnp.arange(EXPERTS, dtype=jnp.int32)[None, :]).astype(
        jnp.float32
    )
    logits = jnp.dot(normed_ffn.astype(jnp.float32), router, precision=highest)
    router_probs = jax.nn.softmax(logits, axis=-1)
    gate = jnp.sum(router_probs * own_onehot, axis=1)
    ffn_rows = lax.all_gather(normed_ffn, "tensor", axis=0, tiled=True)
    slot_of, token_of, filled = expert_slots(route_ids, capacity)
    inputs = jnp.where(filled[..., None], ffn_rows[token_of], jnp.zeros((), jnp.bfloat16))
    expert_in, expert_outw = (
        lax.all_gather(w_in, "dp", axis=0, tiled=True),
        lax.all_gather(w_out, "dp", axis=0, tiled=True),
    )
    pre = jnp.einsum("ecd,def->ecf", inputs, expert_in, preferred_element_type=jnp.float32)
    active = gelu_tanh(pre).astype(jnp.bfloat16)
    expert_out = jnp.einsum("ecf,def->ecd", active, expert_outw, preferred_element_type=jnp.float32)

    def pick_rows(slot_table):
        return slot_table[route_ids, slot_of]

    returned = lax.psum_scatter(pick_rows(expert_out), "tensor", scatter_dimension=0, tiled=True)
    mixed_out = (middle + gate[:, None] * returned).astype(jnp.bfloat16)
    upstream = cotangent.astype(jnp.float32)
    grad_gate = jnp.sum(upstream * returned, axis=1)
    grad_returned = (upstream * gate[:, None]).astype(jnp.bfloat16)
    grad_rows = lax.all_gather(grad_returned, "tensor", axis=0, tiled=True)
    grad_slots = jnp.where(filled[..., None], grad_rows[token_of], jnp.zeros((), jnp.bfloat16))
    grad_active = jnp.einsum(
        "ecd,def->ecf", grad_slots, expert_outw, preferred_element_type=jnp.float32
    )
    gelu_back = jax.vjp(gelu_tanh, pre)[1]
    grad_pre = gelu_back(grad_active)[0].astype(jnp.bfloat16)
    grad_inputs = jnp.einsum(
        "ecf,def->ecd", grad_pre, expert_in, preferred_element_type=jnp.float32
    )
    grad_normed_ffn = lax.psum_scatter(
        pick_rows(grad_inputs), "tensor", scatter_dimension=0, tiled=True
    )
    grad_logits = (grad_gate * gate)[:, None] * (own_onehot - router_probs)
    grad_normed_ffn = grad_normed_ffn + jnp.dot(grad_logits, router.T, precision=highest)
    grad_router = jnp.dot(normed_ffn.astype(jnp.float32).T, grad_logits, precision=highest)
    norm_ffn_back = jax.vjp(rms_scale, middle, gain_ffn)[1]
    grad_middle_norm, grad_gain_ffn = norm_ffn_back(grad_normed_ffn)
    grad_middle = upstream + grad_middle_norm
    grad_branch = lax.all_gather(grad_middle.astype(jnp.bfloat16), "tensor", axis=0, tiled=True)
    grad_attended = jnp.dot(grad_branch, full_output, preferred_element_type=jnp.float32).astype(
        jnp.bfloat16
    )
    offsets = jnp.arange(2 * group_rows + 1, dtype=jnp.int32) - group_rows
    fold_table = (
        bucket_of(offsets)[:, None] == jnp.arange(BUCKETS, dtype=jnp.int32)[None, :]
    ).astype(jnp.float32)
    grad_q_list = []
    grad_k_list = []
    grad_v_list = []
    table_cols = []
    for head_at in range(head_count):
        start_col = head_at * HEAD_DIM
        q_part = query[:, start_col : start_col + HEAD_DIM]
        k_part = key_proj[:, start_col : start_col + HEAD_DIM]
        v_part = value_proj[:, start_col : start_col + HEAD_DIM]
        g_part = grad_attended[:, start_col : start_col + HEAD_DIM]
        probs_f = jnp.exp(head_scores(head_at) - log_totals[head_at][:, None])
        probs_b = probs_f.astype(jnp.bfloat16)
        grad_probs = dot_nt(g_part, v_part)
        row_dot = jnp.sum(grad_probs * probs_f, axis=1, keepdims=True)
        grad_scores = jnp.where(same_seq, probs_f * (grad_probs - row_dot), 0.0).astype(
            jnp.bfloat16
        )
        grad_v_list.append(dot_tn(probs_b, g_part))
        grad_q_list.append(jnp.dot(grad_scores, k_part, preferred_element_type=jnp.float32))
        grad_k_list.append(dot_tn(grad_scores, q_part))
        per_offset = diagonal_sums(grad_scores.astype(jnp.float32))
        table_cols.append(jnp.dot(per_offset, fold_table, precision=highest))
    grad_q = jnp.concatenate(grad_q_list, axis=1).astype(jnp.bfloat16)
    grad_k = jnp.concatenate(grad_k_list, axis=1).astype(jnp.bfloat16)
    grad_v = jnp.concatenate(grad_v_list, axis=1).astype(jnp.bfloat16)
    total_term = dot_nt(grad_q, full_query)
    total_term = total_term + dot_nt(grad_k, full_key)
    grad_normed = lax.psum_scatter(
        (total_term + dot_nt(grad_v, full_value)).astype(jnp.bfloat16),
        "tensor",
        scatter_dimension=0,
        tiled=True,
    ).astype(jnp.float32)
    norm_attn_back = jax.vjp(rms_scale, tok_f32, gain_attn)[1]
    grad_tok_norm, grad_gain_attn = norm_attn_back(grad_normed)
    grad_tokens = grad_middle + grad_tok_norm
    attn_sums = lax.psum_scatter(
        jnp.concatenate(
            [
                dot_tn(gathered, grad_q),
                dot_tn(gathered, grad_k),
                dot_tn(gathered, grad_v),
                dot_tn(grad_branch, attended),
            ],
            axis=1,
        ),
        "dp",
        scatter_dimension=0,
        tiled=True,
    )
    grad_query = attn_sums[:, 0:head_width]
    grad_key = attn_sums[:, head_width : 2 * head_width]
    grad_value = attn_sums[:, 2 * head_width : 3 * head_width]
    grad_output = attn_sums[:, 3 * head_width : 4 * head_width]
    grad_win = jnp.einsum("ecd,ecf->def", inputs, grad_pre, preferred_element_type=jnp.float32)
    grad_wout = jnp.einsum("ecd,ecf->def", grad_slots, active, preferred_element_type=jnp.float32)
    expert_sums = lax.psum_scatter(
        jnp.concatenate([grad_win, grad_wout], axis=2), "dp", scatter_dimension=0, tiled=True
    )
    grad_in = expert_sums[:, :, 0:unit_width]
    grad_out = expert_sums[:, :, unit_width : 2 * unit_width]
    table_grad = lax.dynamic_update_slice_in_dim(
        jnp.zeros(bias_table.shape, jnp.float32),
        jnp.stack(table_cols, axis=1),
        tensor_at * head_count,
        1,
    )
    sum_gain_attn, sum_gain_ffn, sum_table, sum_router = lax.psum(
        (grad_gain_attn, grad_gain_ffn, table_grad, grad_router), ("dp", "tensor")
    )
    return (
        mixed_out,
        grad_tokens,
        sum_gain_attn,
        sum_gain_ffn,
        grad_query,
        grad_key,
        grad_value,
        grad_output,
        sum_table,
        sum_router,
        grad_in,
        grad_out,
    )


def solution(mesh):
    in_specs = (
        P(("dp", "tensor"), None),
        P(),
        P(),
        P("dp", "tensor"),
        P("dp", "tensor"),
        P("dp", "tensor"),
        P("dp", "tensor"),
        P(),
        P(),
        P("dp", None, "tensor"),
        P("dp", None, "tensor"),
        P("dp", None),
        P("dp", None),
        P(("dp", "tensor"), None),
    )
    out_specs = (
        P(("dp", "tensor"), None),
        P(("dp", "tensor"), None),
        P(),
        P(),
        P("dp", "tensor"),
        P("dp", "tensor"),
        P("dp", "tensor"),
        P("dp", "tensor"),
        P(),
        P(),
        P("dp", None, "tensor"),
        P("dp", None, "tensor"),
    )
    return jax.shard_map(
        on_device, mesh=mesh, in_specs=in_specs, out_specs=out_specs, check_vma=False
    )
```

profile of v0, /device:TPU:0, one launch (start us, length us, event | category | flops | bytes accessed | tf_op | source)
XLA Modules:
  0.0 546.5 jit_solution(13677101474761818934)
XLA Ops:
  13.0 11.3 %all_gather.31 = bf16[768,192]{1,0:T(8,128)(2,1)S(1)} all-gather(bf16[96,192]{1,0:T(8,128)(2,1)} %param.19), channel_id=1, replica_groups=mesh['dp'=8,'tensor'=4] {'dp'}, dimensions={0}, use_global_device_ids=true | all-gather | bytes 331776 | tf_op jit(solution)/shard_map/all_gather | solution.py:101
  27.6 19.8 %all_gather.30 = bf16[512,768]{1,0:T(8,128)(2,1)S(1)} all-gather(bf16[128,768]{1,0:T(8,128)(2,1)S(1)} %fusion.40), channel_id=1, replica_groups=mesh['dp'=8,'tensor'=4] {'tensor'}, dimensions={0}, use_global_device_ids=true | all-gather | bytes 983040 | tf_op jit(solution)/shard_map/all_gather | solution.py:108
  47.4 9.3 %all_gather.32 = bf16[768,192]{1,0:T(8,128)(2,1)S(1)} all-gather(bf16[96,192]{1,0:T(8,128)(2,1)} %param.20), channel_id=1, replica_groups=mesh['dp'=8,'tensor'=4] {'dp'}, dimensions={0}, use_global_device_ids=true | all-gather | bytes 331776 | tf_op jit(solution)/shard_map/all_gather | solution.py:102
  58.6 8.9 %all_gather.33 = bf16[768,192]{1,0:T(8,128)(2,1)S(1)} all-gather(bf16[96,192]{1,0:T(8,128)(2,1)S(1)} %copy-done.59), channel_id=1, replica_groups=mesh['dp'=8,'tensor'=4] {'dp'}, dimensions={0}, use_global_device_ids=true | all-gather | bytes 331776 | tf_op jit(solution)/shard_map/all_gather | solution.py:103
  67.9 9.8 %all_gather.34 = bf16[768,192]{1,0:T(8,128)(2,1)S(1)} all-gather(bf16[96,192]{1,0:T(8,128)(2,1)S(1)} %copy-done.60), channel_id=1, replica_groups=mesh['dp'=8,'tensor'=4] {'dp'}, dimensions={0}, use_global_device_ids=true | all-gather | bytes 331776 | tf_op jit(solution)/shard_map/all_gather | solution.py:104
  77.8 21.6 %fusion.126 = (f32[512]{0:T(512)S(1)}, f32[512,512]{0,1:T(8,128)S(1)}) fusion(f32[]{:T(128)} %bitcast.100, f32[]{:T(128)} %bitcast.99, f32[]{:T(128)} %bitcast.98, f32[]{:T(128)} %bitcast.97, f32[]{:T(128)} %bitcast.96, f32[]{:T(128)} %bitcast.95, f32[]{:T(128)} %bitcast.94, f32[]{:T(128)} %bitcast.93, f32[]{:T(128)} %bitcast.92, f32[]{:T(128)} %bitcast.91, ...), kind=kOutput, calls=%fused_computation.278 | convolution fusion | flops 60030464 | bytes 1185920 | tf_op jit(solution)/shard_map/dot_general | solution.py:62
  100.3 21.7 %fusion.127 = (f32[512]{0:T(512)S(1)}, f32[512,512]{0,1:T(8,128)S(1)}) fusion(f32[]{:T(128)} %bitcast.67, f32[]{:T(128)} %bitcast.66, f32[]{:T(128)} %bitcast.65, f32[]{:T(128)} %bitcast.64, f32[]{:T(128)} %bitcast.63, f32[]{:T(128)} %bitcast.62, f32[]{:T(128)} %bitcast.61, f32[]{:T(128)} %bitcast.60, f32[]{:T(128)} %bitcast.59, f32[]{:T(128)} %bitcast.58, ...), kind=kOutput, calls=%fused_computation.279 | convolution fusion | flops 60030464 | bytes 1185920 | tf_op jit(solution)/shard_map/dot_general | solution.py:62
  123.0 22.1 %fusion.128 = (f32[512]{0:T(512)S(1)}, f32[512,512]{0,1:T(8,128)S(1)}) fusion(f32[]{:T(128)} %bitcast.34, f32[]{:T(128)} %bitcast.33, f32[]{:T(128)} %bitcast.32, f32[]{:T(128)} %bitcast.31, f32[]{:T(128)} %bitcast.30, f32[]{:T(128)} %bitcast.29, f32[]{:T(128)} %bitcast.28, f32[]{:T(128)} %bitcast.27, f32[]{:T(128)} %bitcast.26, f32[]{:T(128)} %bitcast.25, ...), kind=kOutput, calls=%fused_computation.280 | convolution fusion | flops 60030464 | bytes 1185920 | tf_op jit(solution)/shard_map/dot_general | solution.py:62
  151.4 24.5 %scatter_fusion = s32[2,384]{1,0:T(2,128)S(1)} fusion(s32[2,384]{1,0:T(2,128)S(1)} %broadcast.234, s32[512]{0:T(512)S(1)} %bitcast.185, s32[512]{0:T(512)S(1)} %iota.42), kind=kCustom, calls=%fused_computation.4 | custom fusion | bytes 10240 | tf_op jit(solution)/shard_map/scatter | solution.py:55
  176.1 6.4 %reduce-scatter.8.cloned.1.call-done = f32[128,768]{1,0:T(8,128)} async-done(((f32[512,768]{1,0:T(8,128)}), f32[128,768]{1,0:T(8,128)}) %reduce-scatter.8.cloned.1.call-update) | async-done | bytes 393232 | tf_op jit(solution)/shard_map/reduce_scatter | solution.py:143
  184.4 18.3 %all_gather.35 = bf16[512,768]{1,0:T(8,128)(2,1)S(1)} all-gather(bf16[128,768]{1,0:T(8,128)(2,1)S(1)} %multiply_convert_fusion.1), channel_id=1, replica_groups=mesh['dp'=8,'tensor'=4] {'tensor'}, dimensions={0}, use_global_device_ids=true | all-gather | bytes 983040 | tf_op jit(solution)/shard_map/all_gather | solution.py:156
  205.6 4.6 fusion.20
  213.8 7.5 %gather_fusion.1 = f32[512,768]{1,0:T(8,128)} fusion(f32[2,384,768]{2,1,0:T(8,128)S(1)} %fusion.116, s32[512]{0:T(512)S(1)} %bitcast.183), kind=kCustom, calls=%fused_computation.1 | custom fusion | bytes 3149824 | tf_op jit(solution)/shard_map/gather | solution.py:168
  223.2 32.8 %reduce-scatter.10.cloned.1.call-done = f32[128,768]{1,0:T(8,128)} async-done(((f32[512,768]{1,0:T(8,128)}), f32[128,768]{1,0:T(8,128)}) %reduce-scatter.10.cloned.1.call-update) | async-done | bytes 393232 | tf_op jit(solution)/shard_map/reduce_scatter | solution.py:170
  257.8 18.1 %all_gather.38 = bf16[512,768]{1,0:T(8,128)(2,1)S(1)} all-gather(bf16[128,768]{1,0:T(8,128)(2,1)S(1)} %get-tuple-element.86), channel_id=1, replica_groups=mesh['dp'=8,'tensor'=4] {'tensor'}, dimensions={0}, use_global_device_ids=true | all-gather | bytes 983040 | tf_op jit(solution)/shard_map/all_gather | solution.py:175
  279.8 4.6 fusion.6
  286.7 7.4 %gather_fusion.3 = f32[512,768]{1,0:T(8,128)} fusion(f32[2,384,768]{2,1,0:T(8,128)S(1)} %fusion.130, s32[512]{0:T(512)S(1)} %bitcast.184), kind=kCustom, calls=%fused_computation.3 | custom fusion | bytes 3149824 | tf_op jit(solution)/shard_map/gather | solution.py:168
  298.1 30.7 %reduce-scatter.12.cloned.1.call-done = f32[128,768]{1,0:T(8,128)} async-done(((f32[512,768]{1,0:T(8,128)}), f32[128,768]{1,0:T(8,128)}) %reduce-scatter.12.cloned.1.call-update) | async-done | bytes 393232 | tf_op jit(solution)/shard_map/reduce_scatter | solution.py:185
  332.1 18.5 %all_gather.39 = bf16[512,768]{1,0:T(8,128)(2,1)S(1)} all-gather(bf16[128,768]{1,0:T(8,128)(2,1)S(1)} %fusion.115), channel_id=1, replica_groups=mesh['dp'=8,'tensor'=4] {'tensor'}, dimensions={0}, use_global_device_ids=true | all-gather | bytes 983040 | tf_op jit(solution)/shard_map/all_gather | solution.py:194
  361.9 3.8 convolution_bitcast_fusion
  365.7 6.6 %pad_maximum_fusion = f32[768,2,1536]{0,2,1:T(8,128)} fusion(f32[768,2,768]{0,2,1:T(8,128)} %convolution_bitcast_fusion, f32[768,2,768]{0,2,1:T(8,128)S(1)} %convolution_bitcast_fusion.1), kind=kLoop, calls=%fused_computation.5 | loop fusion | flops 2359296 | bytes 18874368 | tf_op jit(solution)/shard_map/concatenate | solution.py:259
  372.3 15.0 %copy.68 = f32[768,2,1536]{2,1,0:T(2,128)} copy(f32[768,2,1536]{0,2,1:T(8,128)} %pad_maximum_fusion) | data formatting | bytes 18874368 | tf_op jit(solution)/shard_map/concatenate | solution.py:259
  418.1 40.2 %all-reduce.7 = (f32[768]{0:T(1024)}, f32[768]{0:T(1024)}, f32[32,12]{0,1:T(8,128)}, f32[768,2]{0,1:T(2,128)}) all-reduce(f32[768]{0:T(1024)S(1)} %get-tuple-element.63, f32[768]{0:T(1024)S(1)} %copy-done.65, f32[32,12]{0,1:T(8,128)S(1)} %dynamic_update_slice.3, ...), channel_id=1, replica_groups=mesh['dp'=8,'tensor'=4] {'dp','tensor'}, use_global_device_ids=true, to_apply=%region_29.31 | all-reduce | flops 3456 | bytes 27648 | tf_op jit(solution)/shard_map/psum | solution.py:269
  458.3 74.7 %all-reduce.10.cloned.1.call-done = f32[768,2,1536]{2,1,0:T(2,128)} async-done(((f32[768,2,1536]{2,1,0:T(2,128)}), f32[768,2,1536]{2,1,0:T(2,128)}) %all-reduce.10.cloned.1.call-update) | async-done | bytes 9437200
  (327 shorter events, 90.5 us)
Async XLA Ops:
  8.0 174.4 %reduce-scatter.8.cloned.1.call-start = ((), (), s32[]{:S(2)}) async-start(), calls=%async_computation.5 | async-start | bytes 1966080 | tf_op jit(solution)/shard_map/reduce_scatter | solution.py:143
  57.9 65.1 %copy-start.34 = (bf16[512,192]{0,1:T(8,128)(2,1)}, bf16[512,192]{0,1:T(8,128)(2,1)S(1)}, u32[]{:S(2)}) copy-start(bf16[512,192]{0,1:T(8,128)(2,1)S(1)} %convolution_convert_fusion.2) | copy-start | bytes 589828
  58.3 64.7 %copy-start.32 = (bf16[512,192]{0,1:T(8,128)(2,1)}, bf16[512,192]{0,1:T(8,128)(2,1)S(1)}, u32[]{:S(2)}) copy-start(bf16[512,192]{0,1:T(8,128)(2,1)S(1)} %convolution_convert_fusion.3) | copy-start | bytes 589828
  58.6 64.4 %copy-start.62 = (s32[512]{0:T(512)}, s32[512]{0:T(512)S(1)}, u32[]{:S(2)}) copy-start(s32[512]{0:T(512)S(1)} %convert_reduce_fusion) | copy-start | bytes 6148
  67.9 77.4 %copy-start.36 = (bf16[512,192]{0,1:T(8,128)(2,1)}, bf16[512,192]{0,1:T(8,128)(2,1)S(1)}, u32[]{:S(2)}) copy-start(bf16[512,192]{0,1:T(8,128)(2,1)S(1)} %convolution_convert_fusion.1) | copy-start | bytes 589828
  77.8 67.9 %copy-start.19 = (bf16[768,192]{1,0:T(8,128)(2,1)}, bf16[768,192]{1,0:T(8,128)(2,1)S(1)}, u32[]{:S(2)}) copy-start(bf16[768,192]{1,0:T(8,128)(2,1)S(1)} %all_gather.34) | copy-start | bytes 884740
  100.3 45.3 %copy-start.55 = (bf16[512,64]{0,1:T(8,128)(2,1)}, bf16[512,64]{0,1:T(8,128)(2,1)S(1)}, u32[]{:S(2)}) copy-start(bf16[512,64]{0,1:T(8,128)(2,1)S(1)} %convolution_convert_fusion.7) | copy-start | bytes 196612
  148.4 57.1 %all-gather.3.cloned.1.call-start = ((), (), s32[]{:S(2)}) async-start(), calls=%async_computation.6 | async-start | bytes 2654208 | tf_op jit(solution)/shard_map/all_gather | solution.py:160
  149.3 60.9 %all-gather.5.cloned.1.call-start = ((), (), s32[]{:S(2)}) async-start(), calls=%async_computation.7 | async-start | bytes 2654208 | tf_op jit(solution)/shard_map/all_gather | solution.py:161
  150.1 105.9 %reduce-scatter.10.cloned.1.call-start = ((), (), s32[]{:S(2)}) async-start(), calls=%async_computation.8 | async-start | bytes 1966080 | tf_op jit(solution)/shard_map/reduce_scatter | solution.py:170
  221.3 107.5 %reduce-scatter.12.cloned.1.call-start = ((), (), s32[]{:S(2)}) async-start(), calls=%async_computation.9 | async-start | bytes 1966080 | tf_op jit(solution)/shard_map/reduce_scatter | solution.py:185
  294.1 56.6 %copy-start.20 = (bf16[768,192]{1,0:T(8,128)(2,1)S(1)}, bf16[768,192]{1,0:T(8,128)(2,1)}, u32[]{:S(2)}) copy-start(bf16[768,192]{1,0:T(8,128)(2,1)} %copy-done.19) | copy-start | bytes 884740
  294.1 122.8 %reduce-scatter.14.cloned.1.call-start = ((), (), s32[]{:S(2)}) async-start(), calls=%async_computation.10 | async-start | bytes 983040 | tf_op jit(solution)/shard_map/reduce_scatter | solution.py:229
  358.5 174.4 %all-reduce.10.cloned.1.call-start = ((), (), s32[]{:S(2)}) async-start(), calls=%async_computation.12 | async-start | bytes 18874368
  388.4 148.6 %reduce-scatter.16.cloned.1.call-start = ((), (), s32[]{:S(2)}) async-start(), calls=%async_computation.11 | async-start | bytes 2654208
  415.2 120.6 %copy-start.93 = (f32[128]{0:T(128)S(1)}, f32[128]{0:T(128)}, u32[]{:S(2)}) copy-start(f32[128]{0:T(128)} %copy-done.92) | copy-start | bytes 1540
  415.2 120.6 %copy-start.22 = (f32[128,768]{1,0:T(8,128)S(1)}, f32[128,768]{1,0:T(8,128)}, u32[]{:S(2)}) copy-start(f32[128,768]{1,0:T(8,128)} %copy-done.21) | copy-start | bytes 1179652
  415.2 120.6 %copy-start.81 = (f32[128]{0:T(128)S(1)}, f32[128]{0:T(128)}, u32[]{:S(2)}) copy-start(f32[128]{0:T(128)} %copy-done.79) | copy-start | bytes 1540
  415.3 120.6 %copy-start.85 = (f32[128]{0:T(128)S(1)}, f32[128]{0:T(128)}, u32[]{:S(2)}) copy-start(f32[128]{0:T(128)} %copy-done.84) | copy-start | bytes 1540
  415.3 120.6 %copy-start.88 = (f32[128]{0:T(128)S(1)}, f32[128]{0:T(128)}, u32[]{:S(2)}) copy-start(f32[128]{0:T(128)} %copy-done.87) | copy-start | bytes 1540
  415.4 120.4 %copy-start.27 = (bf16[128,768]{1,0:T(8,128)(2,1)S(1)}, bf16[128,768]{1,0:T(8,128)(2,1)}, u32[]{:S(2)}) copy-start(bf16[128,768]{1,0:T(8,128)(2,1)} %param.29) | copy-start | bytes 589828
  415.4 120.4 %copy-start.28 = (f32[128,768]{1,0:T(8,128)S(1)}, f32[128,768]{1,0:T(8,128)}, u32[]{:S(2)}) copy-start(f32[128,768]{1,0:T(8,128)} %reduce-scatter.10.cloned.1.call-done) | copy-start | bytes 1179652
  416.9 119.0 %copy-start.31 = (bf16[128,768]{1,0:T(8,128)(2,1)S(1)}, bf16[128,768]{1,0:T(8,128)(2,1)}, u32[]{:S(2)}) copy-start(bf16[128,768]{1,0:T(8,128)(2,1)} %reduce-scatter.14.cloned.1.call-done) | copy-start | bytes 589828
  418.1 120.8 %copy-start.1 = (f32[32,12]{0,1:T(8,128)S(1)}, f32[32,12]{0,1:T(8,128)}, u32[]{:S(2)}) copy-start(f32[32,12]{0,1:T(8,128)} %param.23) | copy-start | bytes 4612
  (80 other events, 765.2 us)
Sparse Core Ops, SparseCore 0:
  148.6 33.8 reduce-scatter.7
  221.4 34.5 reduce-scatter.9
  294.2 34.5 reduce-scatter.11
  358.6 22.6 reduce-scatter.13
  403.5 45.7 reduce-scatter.15
Sparse Core Ops, SparseCore 1:
  150.8 27.3 all-gather.2
  180.0 28.8 all-gather.4
  388.5 144.4 all-reduce.9
where the time goes:
time: 552 us; the launch traced here: 546 us
  blocking collectives  154 us (28%)
  waiting for transfers between devices  145 us (26%)
  matrix products  105 us (19%)
  local copies, waits for them, and re-layouts  97.9 us (18%)
  other arithmetic  26 us (5%)
  between operations  17.8 us (3%)
    unnamed x10, waiting for transfers between devices  74.8 us
    dot_general x10, matrix products, dot_nt(): lax.dot_general(left, right, (((1,), (1,)), ((), ())), preferred_element_...  70.2 us
    psum x1, blocking collectives, on_device(): lax.psum((grad_gain_attn, grad_gain_ffn, table_grad, grad_router), ('dp',...  40.2 us
    reduce_scatter x1, waiting for transfers between devices, on_device(): lax.psum_scatter(pick_rows(expert_out), 'tensor', scatter_dimension=0, ti...  32.8 us
    reduce_scatter x1, waiting for transfers between devices, on_device(): lax.psum_scatter(pick_rows(grad_inputs), 'tensor', scatter_dimension=0, t...  30.7 us
    scatter x1, local copies, waits for them, and re-layouts, expert_slots(): token_of = jnp.zeros((EXPERTS, capacity), jnp.int32).at[route_ids, slot_o...  24.5 us
    all_gather x1, blocking collectives, on_device(): gathered = lax.all_gather(normed, 'tensor', axis=0, tiled=True)  19.8 us
    unnamed x205, local copies, waits for them, and re-layouts  18.7 us
  transfers between devices with their start and end apart: 8, of which 4 were waited for; matrix products, arithmetic and copies ran while one was open for 19% of the time, Pallas kernels for 0%

commit v1 on v0

--- a/solution.py
+++ b/solution.py
@@ -1,6 +1,10 @@
+import functools
+
 import jax
 import jax.numpy as jnp
 from jax import lax
+from jax.experimental import pallas as pl
+from jax.experimental.pallas import tpu as pltpu
 from jax.sharding import PartitionSpec as P
 
 HEAD_DIM = 64
@@ -284,6 +288,787 @@
         grad_out,
     )
 
+class Links:
+    def __init__(self, send_sem, recv_sem):
+        self.send_sem, self.recv_sem, self.used = send_sem, recv_sem, 0
+
+    def take(self, count):
+        first = self.used
+        self.used += count
+        return first
+
+    def copy(self, index, src, dst, device):
+        return pltpu.make_async_remote_copy(
+            src_ref=src,
+            dst_ref=dst,
+            send_sem=self.send_sem.at[index],
+            recv_sem=self.recv_sem.at[index],
+            device_id=device,
+            device_id_type=pl.DeviceIdType.MESH,
+        )
+
+
+def line_gather(links, buf, at, count):
+    right, left = links.take(count - 1), links.take(count - 1)
+
+    def to_right(k, shard):
+        return links.copy(right + k, buf.at[shard], buf.at[shard], {"tensor": at + 1})
+
+    def to_left(k, shard):
+        return links.copy(left + k, buf.at[shard], buf.at[shard], {"tensor": at - 1})
+
+    def step(k):
+        @pl.when((at - k >= 0) & (at + 1 < count))
+        def _():
+            if k > 0:
+                to_right(k - 1, at - k).wait_recv()
+            to_right(k, at - k).start()
+
+        @pl.when((at + k < count) & (at >= 1))
+        def _():
+            if k > 0:
+                to_left(k - 1, at + k).wait_recv()
+            to_left(k, at + k).start()
+
+    def finish():
+        for k in range(1, count):
+
+            @pl.when(at == count - 1)
+            def _():
+                to_right(k - 1, at - k).wait_recv()
+
+            @pl.when(at == 0)
+            def _():
+                to_left(k - 1, at + k).wait_recv()
+
+        for k in range(count - 1):
+
+            @pl.when((at - k >= 0) & (at + 1 < count))
+            def _():
+                to_right(k, at - k).wait_send()
+
+            @pl.when((at + k < count) & (at >= 1))
+            def _():
+                to_left(k, at + k).wait_send()
+
+    return step, finish
+
+
+def line_scatter(links, part, send_r, send_l, recv_r, recv_l, at, count):
+    right, left = links.take(count - 1), links.take(count - 1)
+
+    def to_right(slot):
+        return links.copy(right + slot, send_r.at[slot], recv_r.at[slot], {"tensor": at + 1})
+
+    def to_left(slot):
+        return links.copy(left + slot, send_l.at[slot], recv_l.at[slot], {"tensor": at - 1})
+
+    def add(one, other):
+        return (one.astype(jnp.float32) + other.astype(jnp.float32)).astype(jnp.bfloat16)
+
+    def step(k):
+        d = count - 1 - k
+
+        @pl.when(at + d < count)
+        def _():
+            if d < count - 1:
+
+                @pl.when(at > 0)
+                def _():
+                    to_right(d).wait_recv()
+                    send_r[d - 1] = add(part[at + d], recv_r[d])
+
+                @pl.when(at == 0)
+                def _():
+                    send_r[d - 1] = part[at + d]
+            else:
+                send_r[d - 1] = part[at + d]
+            to_right(d - 1).start()
+
+        @pl.when(at - d >= 0)
+        def _():
+            if d < count - 1:
+
+                @pl.when(at < count - 1)
+                def _():
+                    to_left(d).wait_recv()
+                    send_l[d - 1] = add(part[at - d], recv_l[d])
+
+                @pl.when(at == count - 1)
+                def _():
+                    send_l[d - 1] = part[at - d]
+            else:
+                send_l[d - 1] = part[at - d]
+            to_left(d - 1).start()
+
+    def finish(total):
+        total[...] = part[at].astype(jnp.float32)
+
+        @pl.when(at > 0)
+        def _():
+            to_right(0).wait_recv()
+            total[...] += recv_r[0].astype(jnp.float32)
+
+        @pl.when(at < count - 1)
+        def _():
+            to_left(0).wait_recv()
+            total[...] += recv_l[0].astype(jnp.float32)
+
+        for d in range(1, count):
+
+            @pl.when(at + d < count)
+            def _():
+                to_right(d - 1).wait_send()
+
+            @pl.when(at - d >= 0)
+            def _():
+                to_left(d - 1).wait_send()
+
+    return step, finish
+
+
+class ChipGather:
+    def __init__(self, links, own, buf, me, chips):
+        self.links, self.own, self.buf, self.me, self.chips = links, own, buf, me, chips
+        self.chip, self.core = me // 2, me % 2
+        self.mate = self.chip * 2 + 1 - self.core
+        self.first = links.take(2 * chips)
+
+    def peer(self, k):
+        return ((self.chip + k) % self.chips) * 2 + self.core
+
+    def source(self, k):
+        return ((self.chip - k + self.chips) % self.chips) * 2 + self.core
+
+    def send(self, k):
+        target = self.mate if k == 0 else self.peer(k)
+        return self.links.copy(
+            self.first + k, self.own, self.buf.at[self.me], {"dp": target}
+        )
+
+    def hand_over(self, k):
+        shard = self.buf.at[self.source(k)]
+        return self.links.copy(self.first + self.chips + k, shard, shard, {"dp": self.mate})
+
+    def start(self):
+        for k in range(self.chips):
+            self.send(k).start()
+
+    def forward(self):
+        for k in range(1, self.chips):
+            self.send(k).wait_recv()
+            self.hand_over(k).start()
+
+    def finish(self):
+        self.send(0).wait_recv()
+        for k in range(1, self.chips):
+            self.hand_over(k).wait_recv()
+        for k in range(self.chips):
+            self.send(k).wait_send()
+        for k in range(1, self.chips):
+            self.hand_over(k).wait_send()
+
+
+class ChipScatter:
+    def __init__(self, links, part, from_mate, from_chips, me, chips):
+        self.links, self.part, self.from_mate = links, part, from_mate
+        self.summed, self.from_chips, self.chips = from_mate, from_chips, chips
+        self.chip, self.core = me // 2, me % 2
+        self.mate = self.chip * 2 + 1 - self.core
+        self.first = links.take(2 * chips)
+
+    def chip_at(self, k):
+        return (self.chip + k) % self.chips
+
+    def swap(self, k):
+        return self.links.copy(
+            self.first + k,
+            self.part.at[self.chip_at(k) * 2 + 1 - self.core],
+            self.from_mate.at[k],
+            {"dp": self.mate},
+        )
+
+    def cross(self, k):
+        return self.links.copy(
+            self.first + self.chips + k,
+            self.summed.at[k],
+            self.from_chips.at[k - 1],
+            {"dp": self.chip_at(k) * 2 + self.core},
+        )
+
+    def start(self):
+        for k in range(1, self.chips):
+            self.swap(k).start()
+        self.swap(0).start()
+
+    def middle(self):
+        for k in list(range(1, self.chips)) + [0]:
+            self.swap(k).wait_recv()
+            mine = self.part.at[self.chip_at(k) * 2 + self.core]
+
+            @pl.loop(0, self.part.shape[1])
+            def _(row):
+                self.summed[k, row] = (
+                    mine[row].astype(jnp.float32) + self.from_mate[k, row].astype(jnp.float32)
+                ).astype(jnp.bfloat16)
+
+            if k > 0:
+                self.cross(k).start()
+
+    def finish(self, out):
+        for k in range(1, self.chips):
+            self.cross(k).wait_recv()
+
+        @pl.loop(0, self.part.shape[1])
+        def _(row):
+            total = self.summed[0, row].astype(jnp.float32)
+            for k in range(1, self.chips):
+                total = total + self.from_chips[k - 1, row].astype(jnp.float32)
+            out[row] = total
+
+        for k in range(self.chips):
+            self.swap(k).wait_send()
+        for k in range(1, self.chips):
+            self.cross(k).wait_send()
+
+
+def gelu_both(v):
+    c = 0.7978845608028654
+    sq = v * v
+    th = jnp.tanh(c * v * (1.0 + 0.044715 * sq))
+    half = 0.5 * (1.0 + th)
+    slope = half + 0.5 * v * (1.0 - th * th) * c * (1.0 + 3 * 0.044715 * sq)
+    return v * half, slope
+
+
+def rms_back(values, gain, grad):
+    scale = lax.rsqrt(jnp.mean(values * values, axis=-1, keepdims=True) + 1e-06)
+    lifted = grad * gain
+    inner = jnp.mean(lifted * values, axis=-1, keepdims=True)
+    return scale * lifted - values * (scale * scale * scale * inner), jnp.sum(
+        grad * values * scale, axis=0, keepdims=True
+    )
+
+
+def layer_kernel(
+    chips,
+    n_t,
+    heads,
+    tok,
+    cot,
+    gains,
+    attn_own,
+    exp_own,
+    table,
+    router,
+    routes,
+    lengths,
+    mixed_out,
+    gtok_out,
+    small_out,
+    attn_out,
+    exp_out,
+    xg,
+    cg,
+    fg,
+    bg,
+    aw,
+    ew,
+    q3,
+    k3,
+    v3,
+    att,
+    probs,
+    bias,
+    seg_col,
+    pick,
+    slots,
+    gslots,
+    active,
+    slope,
+    gpre,
+    eo,
+    gcols,
+    part_b,
+    part_r,
+    part_g,
+    part_n,
+    pass_buf,
+    total,
+    middle,
+    gmid,
+    gq3,
+    gk3,
+    gv3,
+    gk_acc,
+    gv_acc,
+    diag,
+    gexp,
+    gexp_mate,
+    gexp_chips,
+    gatt,
+    gatt_mate,
+    gatt_chips,
+    small,
+    small_t,
+    small_m,
+    small_in,
+    send_sem,
+    recv_sem,
+):
+    bf, f32 = jnp.bfloat16, jnp.float32
+    me, at = lax.axis_index("dp"), lax.axis_index("tensor")
+    links = Links(send_sem, recv_sem)
+    rows, width = tok.shape
+    size = n_t * rows
+    cap = slots.shape[1]
+    chip, core = me // 2, me % 2
+    mate = chip * 2 + 1 - core
+
+    def chip_peer(k):
+        return ((chip + k) % chips) * 2 + core
+
+    barrier = pltpu.get_barrier_semaphore()
+    for k in range(1, n_t):
+        pl.semaphore_signal(
+            barrier, 1, device_id={"tensor": (at + k) % n_t}, device_id_type=pl.DeviceIdType.MESH
+        )
+    for k in range(chips):
+        pl.semaphore_signal(
+            barrier,
+            1,
+            device_id={"dp": mate if k == 0 else chip_peer(k)},
+            device_id_type=pl.DeviceIdType.MESH,
+        )
+    gain_a, gain_f = gains[0:1, :], gains[1:2, :]
+    x_own = tok[...].astype(f32)
+    xg[at] = rms_scale(x_own, gain_a).astype(bf)
+    cg[at] = cot[...]
+    pl.semaphore_wait(barrier, n_t - 1 + chips)
+
+    x_step, x_end = line_gather(links, xg, at, n_t)
+    c_step, c_end = line_gather(links, cg, at, n_t)
+    f_step, f_end = line_gather(links, fg, at, n_t)
+    b_step, b_end = line_gather(links, bg, at, n_t)
+    attn_w = ChipGather(links, attn_own, aw, me, chips)
+    exp_w = ChipGather(links, exp_own, ew, me, chips)
+    x_step(0)
+    attn_w.start()
+    exp_w.start()
+    aw[me] = attn_own[...]
+    for i in range(4):
+        ew[me, i] = exp_own[i]
+
+    lane = lax.broadcasted_iota(jnp.int32, (BUCKETS, 2 * size), 1)
+    offset = jnp.where(lane < size, lane, lane - 2 * size)
+    hit = (bucket_of(offset) == lax.broadcasted_iota(jnp.int32, (BUCKETS, 2 * size), 0)).astype(f32)
+    for h in range(heads):
+        by_offset = jnp.sum(hit * table[:, h : h + 1], axis=0, keepdims=True)
+        for s in range(n_t):
+            wide = jnp.broadcast_to(by_offset, (rows, 2 * size))
+            bias[h, pl.ds(s * rows, rows)] = pltpu.roll(
+                wide, s * rows, 1, stride=1, stride_axis=0
+            )[:, :size]
+    ends = [lengths[0, 0]]
+    for s in range(1, lengths.shape[1]):
+        ends.append(ends[-1] + lengths[0, s])
+
+    def segments(position):
+        seg = jnp.zeros(position.shape, jnp.int32)
+        for end in ends:
+            seg = seg + (position >= end).astype(jnp.int32)
+        return seg
+
+    seg_row = segments(lax.broadcasted_iota(jnp.int32, (1, size), 1))
+    seg_col[...] = segments(lax.broadcasted_iota(jnp.int32, (size, 1), 0))
+    x_step(1)
+    route = routes[...]
+    onehot = route == lax.broadcasted_iota(jnp.int32, (size, 128), 1)
+    lower = (
+        lax.broadcasted_iota(jnp.int32, (size, size), 1)
+        < lax.broadcasted_iota(jnp.int32, (size, size), 0)
+    ).astype(f32).astype(bf)
+    before = jnp.dot(lower, onehot.astype(f32).astype(bf), preferred_element_type=f32)
+    place = jnp.sum(jnp.where(onehot, before, 0.0), axis=1, keepdims=True).astype(jnp.int32)
+    place = place + route * cap
+    pick[...] = (
+        (place == lax.broadcasted_iota(jnp.int32, (size, EXPERTS * cap), 1)).astype(f32).astype(bf)
+    )
+    for k in range(2, n_t - 1):
+        x_step(k)
+    attn_w.forward()
+    x_end()
+    c_step(0)
+    attn_w.finish()
+
+    def attn_weight(i):
+        return aw[:, i].reshape(width, heads * HEAD_DIM)
+
+    @pl.loop(0, n_t)
+    def _(s):
+        for i, dest in enumerate((q3, k3, v3)):
+            made = jnp.dot(xg[s], attn_weight(i), preferred_element_type=f32).astype(bf)
+            for h in range(heads):
+                dest[h, pl.ds(pl.multiple_of(s * rows, rows), rows)] = made[
+                    :, h * HEAD_DIM : (h + 1) * HEAD_DIM
+                ]
+
+    c_step(1)
+
+    @pl.loop(0, n_t)
+    def _(s):
+        here = pl.ds(pl.multiple_of(s * rows, rows), rows)
+        same = seg_col[here] == seg_row
+        for h in range(heads):
+            scores = dot_nt(q3[h, here], k3[h]) + bias[h, here]
+            scores = jnp.where(same, scores, -1e30)
+            weights = jnp.exp(scores - jnp.max(scores, axis=-1, keepdims=True))
+            p = weights * (1.0 / jnp.sum(weights, axis=-1, keepdims=True))
+            probs[h, here] = p
+            att[here, h * HEAD_DIM : (h + 1) * HEAD_DIM] = jnp.dot(
+                p.astype(bf), v3[h], preferred_element_type=f32
+            ).astype(bf)
+        part_b[s] = dot_nt(att[here], attn_weight(3)).astype(bf)
+
+    def scatter(i, part):
+        return line_scatter(
+            links, part, pass_buf.at[i, 0], pass_buf.at[i, 1], pass_buf.at[i, 2],
+            pass_buf.at[i, 3], at, n_t,
+        )
+
+    br_step, br_end = scatter(0, part_b)
+    gn_step, gn_end = scatter(1, part_g)
+    re_step, re_end = scatter(2, part_r)
+    at_step, at_end = scatter(3, part_n)
+    for k in range(n_t - 1):
+        br_step(k)
+    for k in range(2, n_t - 1):
+        c_step(k)
+    br_end(total)
+    middle[...] = tok[...].astype(f32) + total[...]
+    fg[at] = rms_scale(middle[...], gain_f).astype(bf)
+    f_step(0)
+    c_end()
+    exp_w.forward()
+    for k in range(1, n_t - 1):
+        f_step(k)
+    f_end()
+
+    def block(s):
+        return pl.ds(pl.multiple_of(s * rows, rows), rows)
+
+    @pl.loop(0, n_t)
+    def _(s):
+        values = fg[s].astype(f32)
+        first = jnp.sum(values * router[0:1, :], axis=1, keepdims=True)
+        second = jnp.sum(values * router[1:2, :], axis=1, keepdims=True)
+        most = jnp.maximum(first, second)
+        first, second = jnp.exp(first - most), jnp.exp(second - most)
+        whole = 1.0 / (first + second)
+        first, second = first * whole, second * whole
+        is_second = (routes[block(s)] == 1).astype(f32)
+        gate = jnp.where(is_second > 0.5, second, first)
+        gcols[0, block(s)] = gate
+        gcols[1, block(s)] = 1.0 - is_second - first
+        gcols[2, block(s)] = is_second - second
+        bg[s] = (cg[s].astype(f32) * gate).astype(bf)
+
+    ffn_rows = fg[...].reshape(size, width)
+    grad_rows = bg[...].reshape(size, width)
+    for e in range(EXPERTS):
+        chosen = pick[:, e * cap : (e + 1) * cap]
+        slots[e] = dot_tn(chosen, ffn_rows).astype(bf)
+        gslots[e] = dot_tn(chosen, grad_rows).astype(bf)
+    exp_w.finish()
+    cols = 256
+    units = ew.shape[3]
+    shard_rows = ew.shape[2]
+    half = ew.shape[0] // 2
+    wide_half = half * shard_rows
+
+    def tile(j):
+        return pl.ds(pl.multiple_of(j * cols, cols), cols)
+
+    for e in range(EXPERTS):
+
+        @pl.loop(0, units // cols)
+        def _(j):
+            pre = jnp.dot(
+                slots[e], ew[:, e, :, tile(j)].reshape(width, cols), preferred_element_type=f32
+            )
+            value, rate = gelu_both(pre)
+            active[e, :, tile(j)] = value.astype(bf)
+            slope[e, :, tile(j)] = rate
+
+    for e in range(EXPERTS):
+        for j in range(2):
+            eo[e, :, j * wide_half : (j + 1) * wide_half] = dot_nt(
+                active[e], ew[j * half : (j + 1) * half, 2 + e].reshape(wide_half, units)
+            ).astype(bf)
+
+    @pl.loop(0, n_t)
+    def _(s):
+        back = jnp.dot(
+            pick[block(s)], eo[...].reshape(EXPERTS * cap, width), preferred_element_type=f32
+        )
+        part_r[s] = back.astype(bf)
+        gcols[3, block(s)] = (
+            jnp.sum(cg[s].astype(f32) * back, axis=1, keepdims=True) * gcols[0, block(s)]
+        )
+
+    for e in range(EXPERTS):
+
+        @pl.loop(0, units // cols)
+        def _(j):
+            grad_active = jnp.dot(
+                gslots[e], ew[:, 2 + e, :, tile(j)].reshape(width, cols), preferred_element_type=f32
+            )
+            gpre[e, :, tile(j)] = (grad_active * slope[e, :, tile(j)]).astype(bf)
+
+    for e in range(EXPERTS):
+        for j in range(2):
+            eo[e, :, j * wide_half : (j + 1) * wide_half] = dot_nt(
+                gpre[e], ew[j * half : (j + 1) * half, e].reshape(wide_half, units)
+            ).astype(bf)
+    small[...] = jnp.zeros_like(small)
+
+    @pl.loop(0, n_t)
+    def _(s):
+        back = jnp.dot(
+            pick[block(s)], eo[...].reshape(EXPERTS * cap, width), preferred_element_type=f32
+        )
+        values = fg[s].astype(f32)
+        for e in range(EXPERTS):
+            grad_logit = gcols[3, block(s)] * gcols[1 + e, block(s)]
+            back = back + grad_logit * router[e : e + 1, :]
+            small[2 + e : 3 + e, :] += jnp.sum(values * grad_logit, axis=0, keepdims=True)
+        part_g[s] = back.astype(bf)
+
+    exp_g = ChipScatter(links, gexp, gexp_mate, gexp_chips, me, chips)
+    gn_step(0)
+
+    def weight_grads(left, right, i):
+        @pl.loop(0, units // cols)
+        def _(j):
+            gexp[:, i, :, tile(j)] = (
+                dot_tn(left, right[:, tile(j)]).astype(bf).reshape(2 * half, shard_rows, cols)
+            )
+
+    for e in range(EXPERTS):
+        weight_grads(slots[e], gpre.at[e], e)
+    for k in range(1, n_t - 2):
+        gn_step(k)
+    for e in range(EXPERTS):
+        weight_grads(gslots[e], active.at[e], 2 + e)
+    for k in range(max(1, n_t - 2), n_t - 1):
+        gn_step(k)
+    exp_g.start()
+    gn_end(total)
+    norm_back, gain_part = rms_back(middle[...], gain_f, total[...])
+    small[1:2, :] = gain_part
+    grad_mid = cot[...].astype(f32) + norm_back
+    gmid[...] = grad_mid
+    bg[at] = grad_mid.astype(bf)
+    b_step(0)
+    exp_g.middle()
+    for k in range(1, n_t - 1):
+        b_step(k)
+    b_end()
+    re_step(0)
+
+    diag[...] = jnp.zeros_like(diag)
+    gk_acc[...] = jnp.zeros_like(gk_acc)
+    gv_acc[...] = jnp.zeros_like(gv_acc)
+    mirror = (
+        lax.broadcasted_iota(jnp.int32, (rows, rows), 0)
+        + lax.broadcasted_iota(jnp.int32, (rows, rows), 1)
+        == rows - 1
+    ).astype(f32).astype(bf)
+
+    def attn_back(s):
+        here = block(s)
+        same = seg_col[here] == seg_row
+        grad_att = jnp.dot(bg[s], attn_weight(3), preferred_element_type=f32).astype(bf)
+        for h in range(heads):
+            g_part = grad_att[:, h * HEAD_DIM : (h + 1) * HEAD_DIM]
+            p = probs[h, here]
+            grad_p = dot_nt(g_part, v3[h])
+            row_dot = jnp.sum(grad_p * p, axis=1, keepdims=True)
+            grad_s = jnp.where(same, p * (grad_p - row_dot), 0.0).astype(bf)
+            gv_acc[h] += dot_tn(p.astype(bf), g_part)
+            gk_acc[h] += dot_tn(grad_s, q3[h, here])
+            gq3[here, h * HEAD_DIM : (h + 1) * HEAD_DIM] = jnp.dot(
+                grad_s, k3[h], preferred_element_type=f32
+            ).astype(bf)
+            turned = jnp.dot(mirror, grad_s, preferred_element_type=f32)
+            turned = jnp.concatenate([turned, jnp.zeros((rows, rows), f32)], axis=1)
+            turned = pltpu.roll(turned, 0, 1, stride=1, stride_axis=0)
+            folded = jnp.sum(turned.reshape(rows // 8, 8, size + rows), axis=0)
+            base = pl.multiple_of(size - rows - s * rows, rows)
+            diag[h, :, pl.ds(base, size + rows)] += folded
+
+    @pl.loop(0, n_t // 2)
+    def _(s):
+        attn_back(s)
+
+    for k in range(1, n_t - 2):
+        re_step(k)
+
+    @pl.loop(n_t // 2, n_t)
+    def _(s):
+        attn_back(s)
+
+    for h in range(heads):
+        gk3[:, h * HEAD_DIM : (h + 1) * HEAD_DIM] = gk_acc[h].astype(bf)
+        gv3[:, h * HEAD_DIM : (h + 1) * HEAD_DIM] = gv_acc[h].astype(bf)
+
+    @pl.loop(0, n_t)
+    def _(s):
+        back = dot_nt(gq3[block(s)], attn_weight(0))
+        back = back + dot_nt(gk3[block(s)], attn_weight(1))
+        back = back + dot_nt(gv3[block(s)], attn_weight(2))
+        part_n[s] = back.astype(bf)
+        small[0:1, :] += jnp.sum(back * xg[s].astype(f32), axis=0, keepdims=True)
+
+    at_step(0)
+    small[0:1, :] = small[0:1, :] / gain_a
+    spot = lax.broadcasted_iota(jnp.int32, (2 * size, 128), 0) - (size - 1)
+    fold = (bucket_of(spot) == lax.broadcasted_iota(jnp.int32, (2 * size, 128), 1)).astype(f32)
+    line = lax.broadcasted_iota(jnp.int32, (small.shape[0], 128), 0)
+    for h in range(heads):
+        sums = jnp.dot(diag[h], fold, precision=highest, preferred_element_type=f32)
+        sums = jnp.sum(sums, axis=0, keepdims=True)
+        small[:, 0:128] += jnp.where(line == 4 + at * heads + h, sums, 0.0)
+
+    first = links.take(n_t - 1)
+
+    def small_line(k):
+        return links.copy(first + k - 1, small, small_t.at[k - 1], {"tensor": (at + k) % n_t})
+
+    for k in range(1, n_t):
+        small_line(k).start()
+    att_g = ChipScatter(links, gatt, gatt_mate, gatt_chips, me, chips)
+    normed = xg[...].reshape(size, width)
+    shape = (2 * half, shard_rows, heads * HEAD_DIM)
+    gatt[:, 0] = dot_tn(normed, gq3[...]).astype(bf).reshape(shape)
+    gatt[:, 1] = dot_tn(normed, gk3[...]).astype(bf).reshape(shape)
+    for k in range(1, n_t - 2):
+        at_step(k)
+    gatt[:, 2] = dot_tn(normed, gv3[...]).astype(bf).reshape(shape)
+    gatt[:, 3] = dot_tn(bg[...].reshape(size, width), att[...]).astype(bf).reshape(shape)
+    att_g.start()
+    for k in range(max(1, n_t - 2), n_t - 1):
+        at_step(k)
+    joined = small[...]
+    for k in range(1, n_t):
+        small_line(k).wait_recv()
+        joined = joined + small_t[k - 1]
+    small_m[0] = joined
+    second = links.take(chips)
+    swap = links.copy(second, small_m.at[0], small_in.at[0], {"dp": mate})
+    swap.start()
+    att_g.middle()
+    swap.wait_recv()
+    small_m[1] = small_m[0] + small_in[0]
+
+    def small_chip(k):
+        return links.copy(second + k, small_m.at[1], small_in.at[k], {"dp": chip_peer(k)})
+
+    for k in range(1, chips):
+        small_chip(k).start()
+    for k in range(max(1, n_t - 2), n_t - 1):
+        re_step(k)
+    exp_g.finish(exp_out)
+    at_end(total)
+    tok_back, _ = rms_back(tok[...].astype(f32), gain_a, total[...])
+    gtok_out[...] = gmid[...] + tok_back
+    re_end(total)
+    own_gate = gcols[0, block(at)]
+    mixed_out[...] = (middle[...] + own_gate * total[...]).astype(bf)
+    joined = small_m[1]
+    for k in range(1, chips):
+        small_chip(k).wait_recv()
+        joined = joined + small_in[k]
+    small_out[...] = joined
+    att_g.finish(attn_out)
+    for k in range(1, n_t):
+        small_line(k).wait_send()
+    swap.wait_send()
+    for k in range(1, chips):
+        small_chip(k).wait_send()
+
+
+def fused_layer(
+    tokens, gain_attn, gain_ffn, w_query, w_key, w_value, w_output, bias_table, router,
+    w_in, w_out, routes, lengths, cotangent,
+):
+    bf, f32 = jnp.bfloat16, jnp.float32
+    n_dp, n_t = lax.axis_size("dp"), lax.axis_size("tensor")
+    chips = n_dp // 2
+    rows, width = tokens.shape
+    size = rows * n_t
+    cap = 3 * size // (2 * EXPERTS)
+    shard, head_width = w_query.shape
+    heads = head_width // HEAD_DIM
+    units = w_in.shape[2]
+    all_heads = bias_table.shape[1]
+    small_rows = -(-(4 + all_heads) // 8) * 8
+    attn_own = jnp.stack([w_query, w_key, w_value, w_output])
+    exp_own = jnp.concatenate([w_in.transpose(1, 0, 2), w_out.transpose(1, 0, 2)], axis=0)
+    table = lax.dynamic_slice_in_dim(bias_table, lax.axis_index("tensor") * heads, heads, 1)
+    vm = pl.BlockSpec(memory_space=pltpu.VMEM)
+    V = pltpu.VMEM
+    group = (n_t, rows, width)
+    scratch = [
+        V(group, bf), V(group, bf), V(group, bf), V(group, bf),
+        V((n_dp, 4, shard, head_width), bf), V((n_dp, 4, shard, units), bf),
+        V((heads, size, HEAD_DIM), bf), V((heads, size, HEAD_DIM), bf),
+        V((heads, size, HEAD_DIM), bf),
+        V((size, head_width), bf),
+        V((heads, size, size), f32), V((heads, size, size), f32),
+        V((size, 1), jnp.int32), V((size, EXPERTS * cap), bf),
+        V((EXPERTS, cap, width), bf), V((EXPERTS, cap, width), bf),
+        V((EXPERTS, cap, units), bf), V((EXPERTS, cap, units), f32), V((EXPERTS, cap, units), bf),
+        V((EXPERTS, cap, width), bf), V((4, size, 1), f32),
+        V(group, bf), V(group, bf), V(group, bf), V(group, bf),
+        V((4, 4, n_t - 1, rows, width), bf),
+        V((rows, width), f32), V((rows, width), f32), V((rows, width), f32),
+        V((size, head_width), bf), V((size, head_width), bf), V((size, head_width), bf),
+        V((heads, size, HEAD_DIM), f32), V((heads, size, HEAD_DIM), f32),
+        V((heads, 8, 2 * size), f32),
+        V((n_dp, 4, shard, units), bf), V((chips, 4, shard, units), bf),
+        V((chips - 1, 4, shard, units), bf),
+        V((n_dp, 4, shard, head_width), bf), V((chips, 4, shard, head_width), bf),
+        V((chips - 1, 4, shard, head_width), bf),
+        V((small_rows, width), f32), V((n_t - 1, small_rows, width), f32),
+        V((2, small_rows, width), f32), V((chips, small_rows, width), f32),
+        pltpu.SemaphoreType.DMA((96,)), pltpu.SemaphoreType.DMA((96,)),
+    ]
+    mixed, grad_tok, small, attn_g, exp_g = pl.pallas_call(
+        functools.partial(layer_kernel, chips, n_t, heads),
+        out_shape=(
+            jax.ShapeDtypeStruct((rows, width), bf),
+            jax.ShapeDtypeStruct((rows, width), f32),
+            jax.ShapeDtypeStruct((small_rows, width), f32),
+            jax.ShapeDtypeStruct((4, shard, head_width), f32),
+            jax.ShapeDtypeStruct((4, shard, units), f32),
+        ),
+        in_specs=[vm] * 8 + [pl.BlockSpec(memory_space=pltpu.SMEM)],
+        out_specs=[vm] * 5,
+        scratch_shapes=scratch,
+        compiler_params=pltpu.CompilerParams(
+            collective_id=0, has_side_effects=True, vmem_limit_bytes=60 * 1024 * 1024
+        ),
+    )(
+        tokens, cotangent, jnp.stack([gain_attn, gain_ffn]), attn_own, exp_own, table,
+        router.T, routes, lengths,
+    )
+    return (
+        mixed, grad_tok, small[0], small[1], attn_g[0], attn_g[1], attn_g[2], attn_g[3],
+        small[4 : 4 + all_heads, :BUCKETS].T, small[2:4].T,
+        exp_g[0:2].transpose(1, 0, 2), exp_g[2:4].transpose(1, 0, 2),
+    )
+
 
 def solution(mesh):
     in_specs = (
@@ -316,6 +1101,12 @@
         P("dp", None, "tensor"),
         P("dp", None, "tensor"),
     )
+
+    def layer(*arrays):
+        shard_rows, chips = arrays[3].shape[0], mesh.shape["dp"] // 2
+        fits = shard_rows % 16 == 0 and mesh.shape["dp"] == 2 * chips and chips > 1
+        return (fused_layer if fits else on_device)(*arrays)
+
     return jax.shard_map(
-        on_device, mesh=mesh, in_specs=in_specs, out_specs=out_specs, check_vma=False
-    )
+        layer, mesh=mesh, in_specs=in_specs, out_specs=out_specs, check_vma=False
+    )

time: 552 us -> 164 us (0.30)
  blocking collectives: 154 us -> 0 us
  waiting for transfers between devices: 145 us -> 0 us
  Pallas kernels: 0 us -> 143 us
  matrix products: 105 us -> 0 us
  local copies, waits for them, and re-layouts: 97.9 us -> 16.5 us
  other arithmetic: 26 us -> 3.06 us
  between operations: 17.8 us -> 0.7 us
    pallas_call x0 -> x1, Pallas kernels: none -> 143 us  [fused_layer(): pl.pallas_call(functools.partial(layer_kernel, chips, n_t, heads), out_sh...]
    all_gather x8 -> x0, blocking collectives: 114 us -> none  [the longest x1 19.8 us: on_device(): gathered = lax.all_gather(normed, 'tensor', axis=0, tiled=True)]
    dot_general x42 -> x0, matrix products: 105 us -> none  [the longest x10 70.2 us: dot_nt(): lax.dot_general(left, right, (((1,), (1,)), ((), ())), preferred_element_...]
    unnamed x10 -> x0, waiting for transfers between devices: 74.8 us -> none
    reduce_scatter x4 -> x0, waiting for transfers between devices: 69.9 us -> none  [the longest x1 32.8 us: on_device(): lax.psum_scatter(pick_rows(expert_out), 'tensor', scatter_dimension=0, ti...]
    psum x1 -> x0, blocking collectives: 40.2 us -> none  [on_device(): lax.psum((grad_gain_attn, grad_gain_ffn, table_grad, grad_router), ('dp',...]
    gather x10 -> x0, local copies, waits for them, and re-layouts: 24.7 us -> none  [the longest x2 14.9 us: pick_rows(): return slot_table[route_ids, slot_of]]
    scatter x1 -> x0, local copies, waits for them, and re-layouts: 24.5 us -> none  [expert_slots(): token_of = jnp.zeros((EXPERTS, capacity), jnp.int32).at[route_ids, slot_o...]
  transfers between devices with their start and end apart: 8 -> 0, of which waited for: 4 -> 0; matrix products, arithmetic and copies ran while one was open for 19% -> 0% of each run, Pallas kernels for 0% -> 0%
where the time goes in v1:
time: 164 us; the launch traced here: 163 us
  Pallas kernels  143 us (87%)
  local copies, waits for them, and re-layouts  16.5 us (10%)
  other arithmetic  3.06 us (2%)
    pallas_call x1, Pallas kernels, fused_layer(): pl.pallas_call(functools.partial(layer_kernel, chips, n_t, heads), out_sh...  143 us
    unnamed x12, local copies, waits for them, and re-layouts  6.89 us

profile of v1, /device:TPU:0, one launch (start us, length us, event | category | flops | bytes accessed | tf_op | source)
XLA Modules:
  0.0 163.4 jit_solution(16715113597470092540)
XLA Ops:
  0.6 0.0 copy-start
  0.7 0.7 copy-done
  1.4 0.7 stack.24
  2.0 0.7 stack.25
  2.7 0.6 pad_maximum_fusion.2.gains
  3.3 0.7 copy.32.table
  4.0 1.6 pad_maximum_fusion.1.attn_own
  5.6 1.5 copy.29.routes
  7.2 1.1 copy_bitcast_fusion
  8.3 0.9 pad_maximum_fusion.exp_own
  9.1 143.1 %shard_map.229 = (bf16[128,768]{1,0:T(8,128)(2,1)}, f32[128,768]{1,0:T(8,128)}, f32[16,768]{1,0:T(8,128)}, f32[4,96,192]{2,1,0:T(8,128)}, f32[4,96,768]{2,1,0:T(8,128)}) custom-call(bf16[128,768]{1,0:T(8,128)(2,1)} %tok.1, bf16[128,768]{1,0:T(8,128)(2,1)} %cot.1, f32[2,768]{1,0:T(2,128)} %pad_maximum_fusion.2.gains, ...), custom_call_target="tpu_custom_call" | custom-call | tf_op jit(solution)/shard_map/pallas_call | solution.py:1047
  152.3 1.3 slice_bitcast_fusion.7
  153.6 1.3 slice_bitcast_fusion.6
  154.9 1.4 slice_reduce_fusion
  156.3 1.8 %slice_bitcast_fusion.2 = (f32[96,192]{1,0:T(8,128)}, f32[96,192]{1,0:T(8,128)}, f32[96,192]{1,0:T(8,128)}, f32[96,192]{1,0:T(8,128)}) fusion(f32[4,96,192]{2,1,0:T(8,128)} %get-tuple-element.20), kind=kLoop, calls=%fused_computation.6 | loop fusion | bytes 589824 | tf_op jit(solution)/shard_map/squeeze | solution.py:1067
  158.1 1.3 slice_bitcast_fusion
  159.4 0.0 copy-start.2
  159.5 0.0 copy-start.1
  159.5 1.3 copy.31
  160.7 1.3 copy.30
  162.0 0.0 copy-done.2
  162.0 0.7 copy.37
  162.7 0.0 copy-done.1
  162.7 0.7 copy.38
  (1 shorter events, 0.0 us)
Async XLA Ops:
  0.6 0.7 copy-start
  159.4 2.6 %copy-start.2 = (bf16[128,768]{1,0:T(8,128)(2,1)S(1)}, bf16[128,768]{1,0:T(8,128)(2,1)}, u32[]{:S(2)}) copy-start(bf16[128,768]{1,0:T(8,128)(2,1)} %get-tuple-element.56) | copy-start | bytes 589828
  159.5 3.2 %copy-start.1 = (f32[128,768]{1,0:T(8,128)S(1)}, f32[128,768]{1,0:T(8,128)}, u32[]{:S(2)}) copy-start(f32[128,768]{1,0:T(8,128)} %get-tuple-element.57) | copy-start | bytes 1179652

commit v2 on v1

--- a/solution.py
+++ b/solution.py
@@ -10,6 +10,7 @@
 HEAD_DIM = 64
 EXPERTS = 2
 BUCKETS = 32
+PIECES = 2
 
 
 highest = lax.Precision.HIGHEST
@@ -308,14 +309,14 @@
         )
 
 
-def line_gather(links, buf, at, count):
+def line_gather_piece(links, buf, at, count, here):
     right, left = links.take(count - 1), links.take(count - 1)
 
     def to_right(k, shard):
-        return links.copy(right + k, buf.at[shard], buf.at[shard], {"tensor": at + 1})
+        return links.copy(right + k, buf.at[shard, here], buf.at[shard, here], {"tensor": at + 1})
 
     def to_left(k, shard):
-        return links.copy(left + k, buf.at[shard], buf.at[shard], {"tensor": at - 1})
+        return links.copy(left + k, buf.at[shard, here], buf.at[shard, here], {"tensor": at - 1})
 
     def step(k):
         @pl.when((at - k >= 0) & (at + 1 < count))
@@ -354,14 +355,14 @@
     return step, finish
 
 
-def line_scatter(links, part, send_r, send_l, recv_r, recv_l, at, count):
+def line_scatter_piece(links, part, send_r, send_l, recv_r, recv_l, at, count, here):
     right, left = links.take(count - 1), links.take(count - 1)
 
     def to_right(slot):
-        return links.copy(right + slot, send_r.at[slot], recv_r.at[slot], {"tensor": at + 1})
+        return links.copy(right + slot, send_r.at[slot, here], recv_r.at[slot, here], {"tensor": at + 1})
 
     def to_left(slot):
-        return links.copy(left + slot, send_l.at[slot], recv_l.at[slot], {"tensor": at - 1})
+        return links.copy(left + slot, send_l.at[slot, here], recv_l.at[slot, here], {"tensor": at - 1})
 
     def add(one, other):
         return (one.astype(jnp.float32) + other.astype(jnp.float32)).astype(jnp.bfloat16)
@@ -376,13 +377,13 @@
                 @pl.when(at > 0)
                 def _():
                     to_right(d).wait_recv()
-                    send_r[d - 1] = add(part[at + d], recv_r[d])
+                    send_r[d - 1, here] = add(part[at + d, here], recv_r[d, here])
 
                 @pl.when(at == 0)
                 def _():
-                    send_r[d - 1] = part[at + d]
+                    send_r[d - 1, here] = part[at + d, here]
             else:
-                send_r[d - 1] = part[at + d]
+                send_r[d - 1, here] = part[at + d, here]
             to_right(d - 1).start()
 
         @pl.when(at - d >= 0)
@@ -392,27 +393,27 @@
                 @pl.when(at < count - 1)
                 def _():
                     to_left(d).wait_recv()
-                    send_l[d - 1] = add(part[at - d], recv_l[d])
+                    send_l[d - 1, here] = add(part[at - d, here], recv_l[d, here])
 
                 @pl.when(at == count - 1)
                 def _():
-                    send_l[d - 1] = part[at - d]
+                    send_l[d - 1, here] = part[at - d, here]
             else:
-                send_l[d - 1] = part[at - d]
+                send_l[d - 1, here] = part[at - d, here]
             to_left(d - 1).start()
 
     def finish(total):
-        total[...] = part[at].astype(jnp.float32)
+        total[here] = part[at, here].astype(jnp.float32)
 
         @pl.when(at > 0)
         def _():
             to_right(0).wait_recv()
-            total[...] += recv_r[0].astype(jnp.float32)
+            total[here] += recv_r[0, here].astype(jnp.float32)
 
         @pl.when(at < count - 1)
         def _():
             to_left(0).wait_recv()
-            total[...] += recv_l[0].astype(jnp.float32)
+            total[here] += recv_l[0, here].astype(jnp.float32)
 
         for d in range(1, count):
 
@@ -425,6 +426,34 @@
                 to_left(d - 1).wait_send()
 
     return step, finish
+
+
+def in_pieces(make, rows):
+    height = rows // PIECES
+    made = [make(pl.ds(p * height, height)) for p in range(PIECES)]
+
+    def step(k):
+        for one, _ in made:
+            one(k)
+
+    def finish(*args):
+        for _, last in made:
+            last(*args)
+
+    return step, finish
+
+
+def line_gather(links, buf, at, count):
+    return in_pieces(lambda here: line_gather_piece(links, buf, at, count, here), buf.shape[1])
+
+
+def line_scatter(links, part, send_r, send_l, recv_r, recv_l, at, count):
+    return in_pieces(
+        lambda here: line_scatter_piece(
+            links, part, send_r, send_l, recv_r, recv_l, at, count, here
+        ),
+        part.shape[1],
+    )
 
 
 class ChipGather:
@@ -515,16 +544,14 @@
             if k > 0:
                 self.cross(k).start()
 
-    def finish(self, out):
+    def finish(self, outs):
         for k in range(1, self.chips):
             self.cross(k).wait_recv()
-
-        @pl.loop(0, self.part.shape[1])
-        def _(row):
+        for row, out in enumerate(outs):
             total = self.summed[0, row].astype(jnp.float32)
             for k in range(1, self.chips):
                 total = total + self.from_chips[k - 1, row].astype(jnp.float32)
-            out[row] = total
+            out[...] = total
 
         for k in range(self.chips):
             self.swap(k).wait_send()
@@ -556,18 +583,30 @@
     heads,
     tok,
     cot,
-    gains,
-    attn_own,
-    exp_own,
+    gain_attn,
+    gain_ffn,
+    w_query,
+    w_key,
+    w_value,
+    w_output,
+    w_in,
+    w_out,
     table,
     router,
     routes,
     lengths,
     mixed_out,
     gtok_out,
-    small_out,
-    attn_out,
-    exp_out,
+    gain_attn_out,
+    gain_ffn_out,
+    query_out,
+    key_out,
+    value_out,
+    output_out,
+    bias_out,
+    router_out,
+    in_out,
+    out_out,
     xg,
     cg,
     fg,
@@ -581,6 +620,7 @@
     probs,
     bias,
     seg_col,
+    route_col,
     pick,
     slots,
     gslots,
@@ -621,7 +661,7 @@
     links = Links(send_sem, recv_sem)
     rows, width = tok.shape
     size = n_t * rows
-    cap = slots.shape[1]
+    cap, tail = slots.shape[1], table.shape[0]
     chip, core = me // 2, me % 2
     mate = chip * 2 + 1 - core
 
@@ -640,30 +680,37 @@
             device_id={"dp": mate if k == 0 else chip_peer(k)},
             device_id_type=pl.DeviceIdType.MESH,
         )
-    gain_a, gain_f = gains[0:1, :], gains[1:2, :]
+    width = tok.shape[1]
+    gain_a, gain_f = gain_attn[...].reshape(1, width), gain_ffn[...].reshape(1, width)
     x_own = tok[...].astype(f32)
     xg[at] = rms_scale(x_own, gain_a).astype(bf)
     cg[at] = cot[...]
+    for i, own in enumerate((w_query, w_key, w_value, w_output)):
+        aw[me, i] = own[...]
+    for e in range(EXPERTS):
+        ew[me, e] = w_in[e]
+        ew[me, 2 + e] = w_out[e]
     pl.semaphore_wait(barrier, n_t - 1 + chips)
 
     x_step, x_end = line_gather(links, xg, at, n_t)
     c_step, c_end = line_gather(links, cg, at, n_t)
     f_step, f_end = line_gather(links, fg, at, n_t)
     b_step, b_end = line_gather(links, bg, at, n_t)
-    attn_w = ChipGather(links, attn_own, aw, me, chips)
-    exp_w = ChipGather(links, exp_own, ew, me, chips)
+    attn_w = ChipGather(links, aw.at[me], aw, me, chips)
+    exp_w = ChipGather(links, ew.at[me], ew, me, chips)
     x_step(0)
     attn_w.start()
     exp_w.start()
-    aw[me] = attn_own[...]
-    for i in range(4):
-        ew[me, i] = exp_own[i]
 
     lane = lax.broadcasted_iota(jnp.int32, (BUCKETS, 2 * size), 1)
     offset = jnp.where(lane < size, lane, lane - 2 * size)
     hit = (bucket_of(offset) == lax.broadcasted_iota(jnp.int32, (BUCKETS, 2 * size), 0)).astype(f32)
+    every = jnp.dot(table[...], hit, precision=highest, preferred_element_type=f32)
+    head_row = lax.broadcasted_iota(jnp.int32, every.shape, 0)
     for h in range(heads):
-        by_offset = jnp.sum(hit * table[:, h : h + 1], axis=0, keepdims=True)
+        by_offset = jnp.sum(
+            jnp.where(head_row == at * heads + h, every, 0.0), axis=0, keepdims=True
+        )
         for s in range(n_t):
             wide = jnp.broadcast_to(by_offset, (rows, 2 * size))
             bias[h, pl.ds(s * rows, rows)] = pltpu.roll(
@@ -682,7 +729,9 @@
     seg_row = segments(lax.broadcasted_iota(jnp.int32, (1, size), 1))
     seg_col[...] = segments(lax.broadcasted_iota(jnp.int32, (size, 1), 0))
     x_step(1)
-    route = routes[...]
+    turned = jnp.broadcast_to(routes[...].astype(f32), (128, size)).T
+    route_col[...] = turned[:, 0:1]
+    route = turned.astype(jnp.int32)
     onehot = route == lax.broadcasted_iota(jnp.int32, (size, 128), 1)
     lower = (
         lax.broadcasted_iota(jnp.int32, (size, size), 1)
@@ -690,7 +739,7 @@
     ).astype(f32).astype(bf)
     before = jnp.dot(lower, onehot.astype(f32).astype(bf), preferred_element_type=f32)
     place = jnp.sum(jnp.where(onehot, before, 0.0), axis=1, keepdims=True).astype(jnp.int32)
-    place = place + route * cap
+    place = place + route[:, 0:1] * cap
     pick[...] = (
         (place == lax.broadcasted_iota(jnp.int32, (size, EXPERTS * cap), 1)).astype(f32).astype(bf)
     )
@@ -766,7 +815,7 @@
         first, second = jnp.exp(first - most), jnp.exp(second - most)
         whole = 1.0 / (first + second)
         first, second = first * whole, second * whole
-        is_second = (routes[block(s)] == 1).astype(f32)
+        is_second = route_col[block(s)]
         gate = jnp.where(is_second > 0.5, second, first)
         gcols[0, block(s)] = gate
         gcols[1, block(s)] = 1.0 - is_second - first
@@ -841,7 +890,7 @@
         for e in range(EXPERTS):
             grad_logit = gcols[3, block(s)] * gcols[1 + e, block(s)]
             back = back + grad_logit * router[e : e + 1, :]
-            small[2 + e : 3 + e, :] += jnp.sum(values * grad_logit, axis=0, keepdims=True)
+            small[tail + 2 + e : tail + 3 + e, :] += jnp.sum(values * grad_logit, axis=0, keepdims=True)
         part_g[s] = back.astype(bf)
 
     exp_g = ChipScatter(links, gexp, gexp_mate, gexp_chips, me, chips)
@@ -865,7 +914,7 @@
     exp_g.start()
     gn_end(total)
     norm_back, gain_part = rms_back(middle[...], gain_f, total[...])
-    small[1:2, :] = gain_part
+    small[tail + 1 : tail + 2, :] = gain_part
     grad_mid = cot[...].astype(f32) + norm_back
     gmid[...] = grad_mid
     bg[at] = grad_mid.astype(bf)
@@ -928,17 +977,17 @@
         back = back + dot_nt(gk3[block(s)], attn_weight(1))
         back = back + dot_nt(gv3[block(s)], attn_weight(2))
         part_n[s] = back.astype(bf)
-        small[0:1, :] += jnp.sum(back * xg[s].astype(f32), axis=0, keepdims=True)
+        small[tail : tail + 1, :] += jnp.sum(back * xg[s].astype(f32), axis=0, keepdims=True)
 
     at_step(0)
-    small[0:1, :] = small[0:1, :] / gain_a
+    small[tail : tail + 1, :] = small[tail : tail + 1, :] / gain_a
     spot = lax.broadcasted_iota(jnp.int32, (2 * size, 128), 0) - (size - 1)
     fold = (bucket_of(spot) == lax.broadcasted_iota(jnp.int32, (2 * size, 128), 1)).astype(f32)
     line = lax.broadcasted_iota(jnp.int32, (small.shape[0], 128), 0)
     for h in range(heads):
         sums = jnp.dot(diag[h], fold, precision=highest, preferred_element_type=f32)
         sums = jnp.sum(sums, axis=0, keepdims=True)
-        small[:, 0:128] += jnp.where(line == 4 + at * heads + h, sums, 0.0)
+        small[:, 0:128] += jnp.where(line == at * heads + h, sums, 0.0)
 
     first = links.take(n_t - 1)
 
@@ -978,7 +1027,7 @@
         small_chip(k).start()
     for k in range(max(1, n_t - 2), n_t - 1):
         re_step(k)
-    exp_g.finish(exp_out)
+    exp_g.finish([in_out.at[0], in_out.at[1], out_out.at[0], out_out.at[1]])
     at_end(total)
     tok_back, _ = rms_back(tok[...].astype(f32), gain_a, total[...])
     gtok_out[...] = gmid[...] + tok_back
@@ -989,13 +1038,22 @@
     for k in range(1, chips):
         small_chip(k).wait_recv()
         joined = joined + small_in[k]
-    small_out[...] = joined
-    att_g.finish(attn_out)
+    gain_attn_out[...] = joined[tail : tail + 1]
+    gain_ffn_out[...] = joined[tail + 1 : tail + 2]
+    router_out[...] = joined[tail + 2 : tail + 4]
+    bias_out[...] = joined[0:tail, 0:BUCKETS]
+    att_g.finish([query_out, key_out, value_out, output_out])
     for k in range(1, n_t):
         small_line(k).wait_send()
     swap.wait_send()
     for k in range(1, chips):
         small_chip(k).wait_send()
+
+
+def hand_on(*refs):
+    half = len(refs) // 2
+    for source, dest in zip(refs[:half], refs[half:]):
+        dest[...] = source[...]
 
 
 def fused_layer(
@@ -1013,9 +1071,6 @@
     units = w_in.shape[2]
     all_heads = bias_table.shape[1]
     small_rows = -(-(4 + all_heads) // 8) * 8
-    attn_own = jnp.stack([w_query, w_key, w_value, w_output])
-    exp_own = jnp.concatenate([w_in.transpose(1, 0, 2), w_out.transpose(1, 0, 2)], axis=0)
-    table = lax.dynamic_slice_in_dim(bias_table, lax.axis_index("tensor") * heads, heads, 1)
     vm = pl.BlockSpec(memory_space=pltpu.VMEM)
     V = pltpu.VMEM
     group = (n_t, rows, width)
@@ -1026,7 +1081,7 @@
         V((heads, size, HEAD_DIM), bf),
         V((size, head_width), bf),
         V((heads, size, size), f32), V((heads, size, size), f32),
-        V((size, 1), jnp.int32), V((size, EXPERTS * cap), bf),
+        V((size, 1), jnp.int32), V((size, 1), f32), V((size, EXPERTS * cap), bf),
         V((EXPERTS, cap, width), bf), V((EXPERTS, cap, width), bf),
         V((EXPERTS, cap, units), bf), V((EXPERTS, cap, units), f32), V((EXPERTS, cap, units), bf),
         V((EXPERTS, cap, width), bf), V((4, size, 1), f32),
@@ -1042,31 +1097,41 @@
         V((chips - 1, 4, shard, head_width), bf),
         V((small_rows, width), f32), V((n_t - 1, small_rows, width), f32),
         V((2, small_rows, width), f32), V((chips, small_rows, width), f32),
-        pltpu.SemaphoreType.DMA((96,)), pltpu.SemaphoreType.DMA((96,)),
+        pltpu.SemaphoreType.DMA((256,)), pltpu.SemaphoreType.DMA((256,)),
     ]
-    mixed, grad_tok, small, attn_g, exp_g = pl.pallas_call(
+    wide = jax.ShapeDtypeStruct((1, width), f32)
+    square = jax.ShapeDtypeStruct((shard, head_width), f32)
+    tall = jax.ShapeDtypeStruct((EXPERTS, shard, units), f32)
+    made = pl.pallas_call(
         functools.partial(layer_kernel, chips, n_t, heads),
         out_shape=(
             jax.ShapeDtypeStruct((rows, width), bf),
             jax.ShapeDtypeStruct((rows, width), f32),
-            jax.ShapeDtypeStruct((small_rows, width), f32),
-            jax.ShapeDtypeStruct((4, shard, head_width), f32),
-            jax.ShapeDtypeStruct((4, shard, units), f32),
+            wide, wide, square, square, square, square,
+            jax.ShapeDtypeStruct(bias_table.shape[::-1], f32),
+            jax.ShapeDtypeStruct((EXPERTS, width), f32),
+            tall, tall,
         ),
-        in_specs=[vm] * 8 + [pl.BlockSpec(memory_space=pltpu.SMEM)],
-        out_specs=[vm] * 5,
+        in_specs=[vm] * 13 + [pl.BlockSpec(memory_space=pltpu.SMEM)],
+        out_specs=[vm] * 12,
         scratch_shapes=scratch,
         compiler_params=pltpu.CompilerParams(
             collective_id=0, has_side_effects=True, vmem_limit_bytes=60 * 1024 * 1024
         ),
     )(
-        tokens, cotangent, jnp.stack([gain_attn, gain_ffn]), attn_own, exp_own, table,
-        router.T, routes, lengths,
-    )
+        tokens, cotangent, gain_attn, gain_ffn,
+        w_query, w_key, w_value, w_output, w_in.transpose(1, 0, 2), w_out.transpose(1, 0, 2),
+        bias_table.T, router.T, routes.reshape(1, size), lengths,
+    )
+    made = pl.pallas_call(
+        hand_on,
+        out_shape=tuple(jax.ShapeDtypeStruct(one.shape, one.dtype) for one in made),
+        in_specs=[vm] * 12,
+        out_specs=[vm] * 12,
+    )(*made)
     return (
-        mixed, grad_tok, small[0], small[1], attn_g[0], attn_g[1], attn_g[2], attn_g[3],
-        small[4 : 4 + all_heads, :BUCKETS].T, small[2:4].T,
-        exp_g[0:2].transpose(1, 0, 2), exp_g[2:4].transpose(1, 0, 2),
+        made[0], made[1], made[2][0], made[3][0], *made[4:8], made[8].T, made[9].T,
+        made[10].transpose(1, 0, 2), made[11].transpose(1, 0, 2),
     )
 
 

time: 164 us -> 149 us (0.909)
  local copies, waits for them, and re-layouts: 16.5 us -> 6.35 us
  Pallas kernels: 143 us -> 140 us
  other arithmetic: 3.06 us -> 1.21 us
    pallas_call x1, Pallas kernels: 143 us -> 137 us  [fused_layer(): pl.pallas_call(functools.partial(layer_kernel, chips, n_t, heads), out_sh...]
    transpose x3 -> x0, local copies, waits for them, and re-layouts: 3.95 us -> none  [the longest x1 1.33 us: fused_layer(): small[2:4]]
    pallas_call x0 -> x1, Pallas kernels: none -> 3.03 us  [fused_layer(): pl.pallas_call(hand_on, out_shape=tuple((jax.ShapeDtypeStruct(one.shape,...]
    unnamed x12 -> x8, local copies, waits for them, and re-layouts: 6.89 us -> 4.43 us
    another operation x2 -> x0, other arithmetic: 2.19 us -> none  [the longest x1 1.59 us: fused_layer(): attn_own = jnp.stack([w_query, w_key, w_value, w_output])]
    squeeze x1 -> x0, local copies, waits for them, and re-layouts: 1.78 us -> none  [fused_layer(): attn_g[3]]
where the time goes in v2:
time: 149 us
  Pallas kernels  140 us (94%)
  local copies, waits for them, and re-layouts  6.35 us (4%)
    pallas_call x1, Pallas kernels, fused_layer(): pl.pallas_call(functools.partial(layer_kernel, chips, n_t, heads), out_sh...  137 us
    unnamed x8, local copies, waits for them, and re-layouts  4.43 us
    pallas_call x1, Pallas kernels, fused_layer(): pl.pallas_call(hand_on, out_shape=tuple((jax.ShapeDtypeStruct(one.shape,...  3.03 us

profile of v2, /device:TPU:0, one launch (start us, length us, event | category | flops | bytes accessed | tf_op | source)
XLA Modules:
  0.0 148.6 jit_solution(10735804971239057292)
XLA Ops:
  0.6 1.9 %copy_bitcast_fusion = (bf16[2,96,768]{2,1,0:T(8,128)(2,1)}, bf16[2,96,768]{2,1,0:T(8,128)(2,1)}) fusion(bf16[96,2,768]{2,1,0:T(2,128)(2,1)} %param.24, bf16[96,2,768]{2,1,0:T(2,128)(2,1)} %param.23), kind=kLoop, calls=%fused_computation | loop fusion | bytes 1179648 | tf_op jit(solution)/shard_map/transpose | solution.py:1123
  2.6 137.4 %shard_map.229 = (bf16[128,768]{1,0:T(8,128)(2,1)}, f32[128,768]{1,0:T(8,128)}, f32[1,768]{1,0:T(1,128)}, f32[1,768]{1,0:T(1,128)}, f32[96,192]{1,0:T(8,128)}, /...) custom-call(bf16[128,768]{1,0:T(8,128)(2,1)} %tok.1, ...), custom_call_target="tpu_custom_call" | custom-call | tf_op jit(solution)/shard_map/pallas_call | solution.py:1105
  139.9 3.0 %shard_map.230 = (bf16[128,768]{1,0:T(8,128)(2,1)}, f32[128,768]{1,0:T(8,128)}, f32[1,768]{1,0:T(1,128)}, f32[1,768]{1,0:T(1,128)}, f32[96,192]{1,0:T(8,128)}, /...) custom-call(bf16[128,768]{1,0:T(8,128)(2,1)} %get-tuple-element.36.r, ...), custom_call_target="tpu_custom_call" | custom-call | tf_op jit(solution)/shard_map/pallas_call | solution.py:1126
  143.0 0.0 copy-start.2
  143.0 0.7 copy-done.2
  143.6 0.0 copy-start.1
  143.6 0.6 reduce
  144.3 0.1 copy-done.1
  144.3 0.6 reduce.1
  144.9 0.0 copy-start
  144.9 2.4 %copy.28 = f32[96,2,768]{2,1,0:T(2,128)} copy(f32[96,2,768]{2,0,1:T(8,128)} %bitcast.12) | data formatting | bytes 1179648
  147.3 0.0 copy-done
  147.3 1.3 copy.29
Async XLA Ops:
  143.0 0.7 copy-start.2
  143.6 0.7 copy-start.1
  144.9 2.4 %copy-start = (f32[2,96,768]{2,1,0:T(8,128)S(1)}, f32[2,96,768]{2,1,0:T(8,128)}, u32[]{:S(2)}) copy-start(f32[2,96,768]{2,1,0:T(8,128)} %get-tuple-element.59) | copy-start | bytes 1769476
